TPU v7x, 32 devices: a whole 2x2x4 slice. The times are simulated.
32 devices in a mesh: chan: 16 (over z, y, core), freq: 2 (over x).
Axes of the slice: x: 2, y: 2, z: 4, core: 2. Of those that a mesh axis runs over, the one named last changes fastest.
Arguments:
- spectra: float32 [4, 2, 32, 8192], P('freq', None, 'chan'), parts along dimension 0, may hold values from -6 to 6
- alive_mask: int32 [8192], replicated, may hold values 0 or 1
Outputs:
- cross_band: float32 [16, 9, 4, 512, 1024], P('chan', None, 'freq'), parts along dimension 2
There are 2 independent parts, one for each index of `freq`. A program takes and returns all parts, laid end to end along the dimension named above; an argument that names none is the same for every part. Nothing has to cross between parts.
All inputs are finite; a program needn't handle non-finite values.
Results may differ from a plain program's by a relative error of at most 0.0034.
Values may be sent and summed in bfloat16 or wider, within the bound.
A program may use at most 128 MiB of HBM per device.

v0:
```python
import jax
import jax.numpy as jnp
from jax import lax
from jax.sharding import PartitionSpec as P


def from_behind(block, axis, distance):
    devices = range(lax.axis_size(axis))
    route = [((i - distance) % len(devices), i) for i in devices]
    return lax.ppermute(block, axis, route)


def cross_block(own_stacked, partner_block, windows):
    product = jnp.einsum(
        "fjw,fiw->fji", partner_block, own_stacked, preferred_element_type=jnp.float32
    )
    return product / windows


def shards(spectra, alive_mask):
    channel_devices = lax.axis_size("chan")
    groups = spectra.shape[0]
    block_width = spectra.shape[3] // channel_devices
    windows = spectra.shape[2] * channel_devices
    lag_count = channel_devices // 2 + 1
    real_part = spectra[:, 0]
    imag_part = spectra[:, 1]
    magnitude = jnp.sqrt(real_part * real_part + imag_part * imag_part)
    factor = alive_mask.astype(jnp.float32)[None, None, :] / jnp.maximum(magnitude, 1.0)
    whitened = (spectra * factor[:, None]).astype(jnp.bfloat16)
    regrouped = lax.all_to_all(whitened, "chan", split_axis=3, concat_axis=2, tiled=True)
    own_block = jnp.transpose(regrouped.reshape(groups, 2 * windows, block_width), (0, 2, 1))
    turned = jnp.concatenate([own_block[:, :, windows:], -own_block[:, :, :windows]], axis=2)
    own_stacked = jnp.concatenate([own_block, turned], axis=1)
    empty_band = jnp.zeros((lag_count, groups, block_width, 2 * block_width), jnp.float32)
    start_band = lax.dynamic_update_index_in_dim(
        empty_band, cross_block(own_stacked, own_block, windows), 0, 0
    )

    def four_steps(turn, carry):
        visitor, band = carry
        for repeat in range(4):
            visitor = from_behind(visitor, "chan", 1)
            band = lax.dynamic_update_index_in_dim(
                band, cross_block(own_stacked, visitor, windows), 1 + 4 * turn + repeat, 0
            )
        return (visitor, band)

    visitor, cross_band = lax.fori_loop(
        0, channel_devices // 8, four_steps, (own_block, start_band)
    )
    return cross_band[None]


def solution(mesh):
    return jax.shard_map(
        shards,
        mesh=mesh,
        in_specs=(P("freq", None, "chan", None), P()),
        out_specs=P("chan", None, "freq", None, None),
        check_vma=False,
    )
```

profile of v0, /device:TPU:0, one launch (start us, length us, event | category | flops | bytes accessed | tf_op | source)
XLA Modules:
  0.0 159.3 jit_solution(11767557847769686998)
XLA Ops:
  0.0 0.8 convert_element_type.6
  0.8 1.2 divide_bitcast_fusion
  2.0 1.1 multiply_convert_fusion
  3.0 12.9 %copy.6 = bf16[2,2,2,8192]{2,1,0,3:T(2,128)(2,1)} copy(bf16[2,2,2,8192]{3,2,1,0:T(2,128)(2,1)S(1)} %multiply_convert_fusion) | data formatting | bytes 262144 | tf_op jit(solution)/shard_map/convert_element_type | solution.py:30
  15.9 13.7 %reshape.6 = bf16[16,2,2048]{2,1,0:T(2,128)(2,1)} reshape(bf16[8192,2,2,2]{3,2,1,0:T(2,128)(2,1)} %bitcast.51) | data formatting | bytes 262144
  29.7 7.4 %all-to-all-start = ((bf16[16,2,2048]{2,1,0:T(2,128)(2,1)}), bf16[16,2,2048]{2,1,0:T(2,128)(2,1)S(1)}, u32[]{:S(2)}, u32[]{:S(2)}) async-start(bf16[16,2,2048]{2,1,0:T(2,128)(2,1)} %reshape.6), calls=%async_computation | async-start | bytes 262144 | tf_op jit(solution)/shard_map/all_to_all | solution.py:31
  37.1 7.9 %all-to-all-done = bf16[16,2,2048]{2,1,0:T(2,128)(2,1)S(1)} async-done(((bf16[16,2,2048]{2,1,0:T(2,128)(2,1)}), bf16[16,2,2048]{2,1,0:T(2,128)(2,1)S(1)}, u32[]{:S(2)}, u32[]{:S(2)}) %all-to-all-start) | async-done | bytes 131104 | tf_op jit(solution)/shard_map/all_to_all | solution.py:31
  45.0 19.0 %reshape.7 = bf16[8192,2,2,2]{3,2,1,0:T(2,128)(2,1)} reshape(bf16[16,2,2048]{2,1,0:T(2,128)(2,1)S(1)} %all-to-all-done) | data formatting | bytes 262144
  64.0 19.2 %copy.7 = bf16[2,2,2,16,512]{4,2,3,1,0:T(2,128)(2,1)S(1)} copy(bf16[2,2,2,16,512]{2,1,0,4,3:T(2,128)(2,1)} %bitcast.52) | data formatting | bytes 262144 | tf_op jit(solution)/shard_map/all_to_all | solution.py:31
  83.3 0.1 reshape.5
  83.4 0.7 multiply_bitcast_fusion
  84.2 12.9 %dynamic_update_slice.57 = f32[9,2,512,1024]{3,2,1,0:T(8,128)} pad(f32[1,2,512,1024]{3,2,1,0:T(8,128)S(1)} %multiply_bitcast_fusion, f32[]{:T(128)} %constant.127.clone.1), padding=0_8x0_0x0_0x0_0 | pad | bytes 41943044 | tf_op jit(solution)/shard_map/jit(dynamic_update_index_in_dim)/dynamic_update_slice | solution.py:36
  97.0 62.2 %while.19 = (s32[]{:T(128)}, bf16[2,512,64]{1,2,0:T(8,128)(2,1)S(1)}, f32[9,2,512,1024]{3,2,1,0:T(8,128)}, bf16[2,1024,64]{1,2,0:T(8,128)(2,1)S(1)}, s32[]{:T(12...) while((s32[]{:T(128)}, ...), condition=%wide.region_1.2_spmd, body=%wide.region_0.1_spmd.sunk | while | flops 541065216 | bytes 20447728 | solution.py:49
  97.0 0.0 collective-permute-start
  97.1 7.1 %collective-permute-done = bf16[2,512,64]{1,2,0:T(8,128)(2,1)S(1)} collective-permute-done((bf16[2,512,64]{1,2,0:T(8,128)(2,1)S(1)}, bf16[2,512,64]{1,2,0:T(8,128)(2,1)S(1)}, u32[]{:S(2)}, u32[]{:S(2)}) %collective-permute-start) | collective-permute-done | bytes 131104 | tf_op jit(solution)/shard_map/while/body/eval_jaxpr/ppermute | solution.py:10
  104.1 0.0 collective-permute-start.1
  104.1 2.8 %bitcast_dynamic-update-slice_fusion.8 = f32[9,2,512,1024]{3,2,1,0:T(8,128)} fusion(f32[9,2,512,1024]{3,2,1,0:T(8,128)} %get-tuple-element.202, s32[]{:T(128)S(6)} %select_n.59, bf16[2,512,64]{1,2,0:T(8,128)(2,1)S(1)} %collective-permute-done, bf16[2,1024,64]{1,2,0:T(8,128)(2,1)S(1)} %get-tuple-element.216), kind=kOutput, calls=%fused_computation.3.clone.1 | convolution fusion | flops 135266304 | bytes 4587524 | tf_op jit(solution)/shard_map/while/body/eval_jaxpr/fjw,fiw->fji/dot_general | solution.py:14
  106.9 4.3 %collective-permute-done.1 = bf16[2,512,64]{1,2,0:T(8,128)(2,1)S(1)} collective-permute-done((bf16[2,512,64]{1,2,0:T(8,128)(2,1)S(1)}, bf16[2,512,64]{1,2,0:T(8,128)(2,1)S(1)}, u32[]{:S(2)}, u32[]{:S(2)}) %collective-permute-start.1) | collective-permute-done | bytes 131104 | tf_op jit(solution)/shard_map/while/body/eval_jaxpr/ppermute | solution.py:10
  111.2 0.0 collective-permute-start.2
  111.2 2.8 %bitcast_dynamic-update-slice_fusion.9 = f32[9,2,512,1024]{3,2,1,0:T(8,128)} fusion(f32[9,2,512,1024]{3,2,1,0:T(8,128)} %bitcast_dynamic-update-slice_fusion.8, s32[]{:T(128)S(6)} %select_n.60, bf16[2,512,64]{1,2,0:T(8,128)(2,1)S(1)} %collective-permute-done.1, bf16[2,1024,64]{1,2,0:T(8,128)(2,1)S(1)} %get-tuple-element.216), kind=kOutput, calls=%fused_computation.2.clone.1 | convolution fusion | flops 135266304 | bytes 4587524 | tf_op jit(solution)/shard_map/while/body/eval_jaxpr/fjw,fiw->fji/dot_general | solution.py:14
  114.0 4.3 %collective-permute-done.2 = bf16[2,512,64]{1,2,0:T(8,128)(2,1)S(1)} collective-permute-done((bf16[2,512,64]{1,2,0:T(8,128)(2,1)S(1)}, bf16[2,512,64]{1,2,0:T(8,128)(2,1)S(1)}, u32[]{:S(2)}, u32[]{:S(2)}) %collective-permute-start.2) | collective-permute-done | bytes 131104 | tf_op jit(solution)/shard_map/while/body/eval_jaxpr/ppermute | solution.py:10
  118.3 0.0 collective-permute-start.3
  118.3 2.8 %bitcast_dynamic-update-slice_fusion.10 = f32[9,2,512,1024]{3,2,1,0:T(8,128)} fusion(f32[9,2,512,1024]{3,2,1,0:T(8,128)} %bitcast_dynamic-update-slice_fusion.9, s32[]{:T(128)S(6)} %select_n.61, bf16[2,512,64]{1,2,0:T(8,128)(2,1)S(1)} %collective-permute-done.2, bf16[2,1024,64]{1,2,0:T(8,128)(2,1)S(1)} %get-tuple-element.216), kind=kOutput, calls=%fused_computation.1.clone.1 | convolution fusion | flops 135266304 | bytes 4587524 | tf_op jit(solution)/shard_map/while/body/eval_jaxpr/fjw,fiw->fji/dot_general | solution.py:14
  121.1 4.3 %collective-permute-done.3 = bf16[2,512,64]{1,2,0:T(8,128)(2,1)S(1)} collective-permute-done((bf16[2,512,64]{1,2,0:T(8,128)(2,1)S(1)}, bf16[2,512,64]{1,2,0:T(8,128)(2,1)S(1)}, u32[]{:S(2)}, u32[]{:S(2)}) %collective-permute-start.3) | collective-permute-done | bytes 131104 | tf_op jit(solution)/shard_map/while/body/eval_jaxpr/ppermute | solution.py:10
  125.4 2.8 %bitcast_dynamic-update-slice_fusion.11 = f32[9,2,512,1024]{3,2,1,0:T(8,128)} fusion(f32[9,2,512,1024]{3,2,1,0:T(8,128)} %bitcast_dynamic-update-slice_fusion.10, s32[]{:T(128)S(6)} %select_n.62, bf16[2,512,64]{1,2,0:T(8,128)(2,1)S(1)} %collective-permute-done.3, bf16[2,1024,64]{1,2,0:T(8,128)(2,1)S(1)} %get-tuple-element.216), kind=kOutput, calls=%fused_computation.clone.1 | convolution fusion | flops 135266304 | bytes 4587524 | tf_op jit(solution)/shard_map/while/body/eval_jaxpr/fjw,fiw->fji/dot_general | solution.py:14
  128.2 0.0 collective-permute-start
  128.2 7.1 %collective-permute-done = bf16[2,512,64]{1,2,0:T(8,128)(2,1)S(1)} collective-permute-done((bf16[2,512,64]{1,2,0:T(8,128)(2,1)S(1)}, bf16[2,512,64]{1,2,0:T(8,128)(2,1)S(1)}, u32[]{:S(2)}, u32[]{:S(2)}) %collective-permute-start) | collective-permute-done | bytes 131104 | tf_op jit(solution)/shard_map/while/body/eval_jaxpr/ppermute | solution.py:10
  135.3 0.0 collective-permute-start.1
  135.3 2.8 %bitcast_dynamic-update-slice_fusion.8 = f32[9,2,512,1024]{3,2,1,0:T(8,128)} fusion(f32[9,2,512,1024]{3,2,1,0:T(8,128)} %get-tuple-element.202, s32[]{:T(128)S(6)} %select_n.59, bf16[2,512,64]{1,2,0:T(8,128)(2,1)S(1)} %collective-permute-done, bf16[2,1024,64]{1,2,0:T(8,128)(2,1)S(1)} %get-tuple-element.216), kind=kOutput, calls=%fused_computation.3.clone.1 | convolution fusion | flops 135266304 | bytes 4587524 | tf_op jit(solution)/shard_map/while/body/eval_jaxpr/fjw,fiw->fji/dot_general | solution.py:14
  138.0 4.3 %collective-permute-done.1 = bf16[2,512,64]{1,2,0:T(8,128)(2,1)S(1)} collective-permute-done((bf16[2,512,64]{1,2,0:T(8,128)(2,1)S(1)}, bf16[2,512,64]{1,2,0:T(8,128)(2,1)S(1)}, u32[]{:S(2)}, u32[]{:S(2)}) %collective-permute-start.1) | collective-permute-done | bytes 131104 | tf_op jit(solution)/shard_map/while/body/eval_jaxpr/ppermute | solution.py:10
  142.3 0.0 collective-permute-start.2
  142.4 2.8 %bitcast_dynamic-update-slice_fusion.9 = f32[9,2,512,1024]{3,2,1,0:T(8,128)} fusion(f32[9,2,512,1024]{3,2,1,0:T(8,128)} %bitcast_dynamic-update-slice_fusion.8, s32[]{:T(128)S(6)} %select_n.60, bf16[2,512,64]{1,2,0:T(8,128)(2,1)S(1)} %collective-permute-done.1, bf16[2,1024,64]{1,2,0:T(8,128)(2,1)S(1)} %get-tuple-element.216), kind=kOutput, calls=%fused_computation.2.clone.1 | convolution fusion | flops 135266304 | bytes 4587524 | tf_op jit(solution)/shard_map/while/body/eval_jaxpr/fjw,fiw->fji/dot_general | solution.py:14
  145.1 4.3 %collective-permute-done.2 = bf16[2,512,64]{1,2,0:T(8,128)(2,1)S(1)} collective-permute-done((bf16[2,512,64]{1,2,0:T(8,128)(2,1)S(1)}, bf16[2,512,64]{1,2,0:T(8,128)(2,1)S(1)}, u32[]{:S(2)}, u32[]{:S(2)}) %collective-permute-start.2) | collective-permute-done | bytes 131104 | tf_op jit(solution)/shard_map/while/body/eval_jaxpr/ppermute | solution.py:10
  149.4 0.0 collective-permute-start.3
  149.4 2.8 %bitcast_dynamic-update-slice_fusion.10 = f32[9,2,512,1024]{3,2,1,0:T(8,128)} fusion(f32[9,2,512,1024]{3,2,1,0:T(8,128)} %bitcast_dynamic-update-slice_fusion.9, s32[]{:T(128)S(6)} %select_n.61, bf16[2,512,64]{1,2,0:T(8,128)(2,1)S(1)} %collective-permute-done.2, bf16[2,1024,64]{1,2,0:T(8,128)(2,1)S(1)} %get-tuple-element.216), kind=kOutput, calls=%fused_computation.1.clone.1 | convolution fusion | flops 135266304 | bytes 4587524 | tf_op jit(solution)/shard_map/while/body/eval_jaxpr/fjw,fiw->fji/dot_general | solution.py:14
  152.2 4.3 %collective-permute-done.3 = bf16[2,512,64]{1,2,0:T(8,128)(2,1)S(1)} collective-permute-done((bf16[2,512,64]{1,2,0:T(8,128)(2,1)S(1)}, bf16[2,512,64]{1,2,0:T(8,128)(2,1)S(1)}, u32[]{:S(2)}, u32[]{:S(2)}) %collective-permute-start.3) | collective-permute-done | bytes 131104 | tf_op jit(solution)/shard_map/while/body/eval_jaxpr/ppermute | solution.py:10
  156.5 2.8 %bitcast_dynamic-update-slice_fusion.11 = f32[9,2,512,1024]{3,2,1,0:T(8,128)} fusion(f32[9,2,512,1024]{3,2,1,0:T(8,128)} %bitcast_dynamic-update-slice_fusion.10, s32[]{:T(128)S(6)} %select_n.62, bf16[2,512,64]{1,2,0:T(8,128)(2,1)S(1)} %collective-permute-done.3, bf16[2,1024,64]{1,2,0:T(8,128)(2,1)S(1)} %get-tuple-element.216), kind=kOutput, calls=%fused_computation.clone.1 | convolution fusion | flops 135266304 | bytes 4587524 | tf_op jit(solution)/shard_map/while/body/eval_jaxpr/fjw,fiw->fji/dot_general | solution.py:14
  (2 shorter events, 0.0 us)
Async XLA Ops:
  29.7 15.3 %all-to-all-start = ((bf16[16,2,2048]{2,1,0:T(2,128)(2,1)}), bf16[16,2,2048]{2,1,0:T(2,128)(2,1)S(1)}, u32[]{:S(2)}, u32[]{:S(2)}) async-start(bf16[16,2,2048]{2,1,0:T(2,128)(2,1)} %reshape.6), calls=%async_computation | async-start | bytes 262144 | tf_op jit(solution)/shard_map/all_to_all | solution.py:31
  97.0 7.1 %collective-permute-start = (bf16[2,512,64]{1,2,0:T(8,128)(2,1)S(1)}, bf16[2,512,64]{1,2,0:T(8,128)(2,1)S(1)}, u32[]{:S(2)}, u32[]{:S(2)}) collective-permute-start(bf16[2,512,64]{1,2,0:T(8,128)(2,1)S(1)} %get-tuple-element.201), channel_id=1, source_target_pairs={{30,0},{0,2},{2,4},{4,6},{6,8},{8,10},{10,12},{12,14},{14,16},{16,... | collective-permute-start | bytes 393224 | tf_op jit(solution)/shard_map/while/body/eval_jaxpr/ppermute | solution.py:10
  104.1 7.1 %collective-permute-start.1 = (bf16[2,512,64]{1,2,0:T(8,128)(2,1)S(1)}, bf16[2,512,64]{1,2,0:T(8,128)(2,1)S(1)}, u32[]{:S(2)}, u32[]{:S(2)}) collective-permute-start(bf16[2,512,64]{1,2,0:T(8,128)(2,1)S(1)} %collective-permute-done), channel_id=1, source_target_pairs={{30,0},{0,2},{2,4},{4,6},{6,8},{8,10},{10,12},{12,14},{14,16},{16,... | collective-permute-start | bytes 393224 | tf_op jit(solution)/shard_map/while/body/eval_jaxpr/ppermute | solution.py:10
  111.2 7.1 %collective-permute-start.2 = (bf16[2,512,64]{1,2,0:T(8,128)(2,1)S(1)}, bf16[2,512,64]{1,2,0:T(8,128)(2,1)S(1)}, u32[]{:S(2)}, u32[]{:S(2)}) collective-permute-start(bf16[2,512,64]{1,2,0:T(8,128)(2,1)S(1)} %collective-permute-done.1), channel_id=1, source_target_pairs={{30,0},{0,2},{2,4},{4,6},{6,8},{8,10},{10,12},{12,14},{14,16},{16,... | collective-permute-start | bytes 393224 | tf_op jit(solution)/shard_map/while/body/eval_jaxpr/ppermute | solution.py:10
  118.3 7.1 %collective-permute-start.3 = (bf16[2,512,64]{1,2,0:T(8,128)(2,1)S(1)}, bf16[2,512,64]{1,2,0:T(8,128)(2,1)S(1)}, u32[]{:S(2)}, u32[]{:S(2)}) collective-permute-start(bf16[2,512,64]{1,2,0:T(8,128)(2,1)S(1)} %collective-permute-done.2), channel_id=1, source_target_pairs={{30,0},{0,2},{2,4},{4,6},{6,8},{8,10},{10,12},{12,14},{14,16},{16,... | collective-permute-start | bytes 393224 | tf_op jit(solution)/shard_map/while/body/eval_jaxpr/ppermute | solution.py:10
  128.2 7.1 %collective-permute-start = (bf16[2,512,64]{1,2,0:T(8,128)(2,1)S(1)}, bf16[2,512,64]{1,2,0:T(8,128)(2,1)S(1)}, u32[]{:S(2)}, u32[]{:S(2)}) collective-permute-start(bf16[2,512,64]{1,2,0:T(8,128)(2,1)S(1)} %get-tuple-element.201), channel_id=1, source_target_pairs={{30,0},{0,2},{2,4},{4,6},{6,8},{8,10},{10,12},{12,14},{14,16},{16,... | collective-permute-start | bytes 393224 | tf_op jit(solution)/shard_map/while/body/eval_jaxpr/ppermute | solution.py:10
  135.3 7.1 %collective-permute-start.1 = (bf16[2,512,64]{1,2,0:T(8,128)(2,1)S(1)}, bf16[2,512,64]{1,2,0:T(8,128)(2,1)S(1)}, u32[]{:S(2)}, u32[]{:S(2)}) collective-permute-start(bf16[2,512,64]{1,2,0:T(8,128)(2,1)S(1)} %collective-permute-done), channel_id=1, source_target_pairs={{30,0},{0,2},{2,4},{4,6},{6,8},{8,10},{10,12},{12,14},{14,16},{16,... | collective-permute-start | bytes 393224 | tf_op jit(solution)/shard_map/while/body/eval_jaxpr/ppermute | solution.py:10
  142.3 7.1 %collective-permute-start.2 = (bf16[2,512,64]{1,2,0:T(8,128)(2,1)S(1)}, bf16[2,512,64]{1,2,0:T(8,128)(2,1)S(1)}, u32[]{:S(2)}, u32[]{:S(2)}) collective-permute-start(bf16[2,512,64]{1,2,0:T(8,128)(2,1)S(1)} %collective-permute-done.1), channel_id=1, source_target_pairs={{30,0},{0,2},{2,4},{4,6},{6,8},{8,10},{10,12},{12,14},{14,16},{16,... | collective-permute-start | bytes 393224 | tf_op jit(solution)/shard_map/while/body/eval_jaxpr/ppermute | solution.py:10
  149.4 7.1 %collective-permute-start.3 = (bf16[2,512,64]{1,2,0:T(8,128)(2,1)S(1)}, bf16[2,512,64]{1,2,0:T(8,128)(2,1)S(1)}, u32[]{:S(2)}, u32[]{:S(2)}) collective-permute-start(bf16[2,512,64]{1,2,0:T(8,128)(2,1)S(1)} %collective-permute-done.2), channel_id=1, source_target_pairs={{30,0},{0,2},{2,4},{4,6},{6,8},{8,10},{10,12},{12,14},{14,16},{16,... | collective-permute-start | bytes 393224 | tf_op jit(solution)/shard_map/while/body/eval_jaxpr/ppermute | solution.py:10
where the time goes:
time: 160 us; the launch traced here: 159 us
  local copies, waits for them, and re-layouts  77.9 us (49%)
  waiting for transfers between devices  48.1 us (30%)
  matrix products  22.8 us (14%)
  starting transfers between devices  7.41 us (5%)
  other arithmetic  3.06 us (2%)
    ppermute x8, waiting for transfers between devices, from_behind(): return lax.ppermute(block, axis, route)  40.1 us
    unnamed x2, local copies, waits for them, and re-layouts  32.8 us
    dot_general x9, matrix products, cross_block(): jnp.einsum('fjw,fiw->fji', partner_block, own_stacked, preferred_element_...  22.8 us
    all_to_all x1, local copies, waits for them, and re-layouts, shards(): lax.all_to_all(whitened, 'chan', split_axis=3, concat_axis=2, tiled=True)  19.2 us
    convert_element_type x1, local copies, waits for them, and re-layouts, shards(): whitened = (spectra * factor[:, None]).astype(jnp.bfloat16)  12.9 us
    dynamic_update_slice x1, local copies, waits for them, and re-layouts, shards(): lax.dynamic_update_index_in_dim(empty_band, cross_block(own_stacked, own_...  12.9 us
    all_to_all x1, waiting for transfers between devices, shards(): lax.all_to_all(whitened, 'chan', split_axis=3, concat_axis=2, tiled=True)  7.94 us
    all_to_all x1, starting transfers between devices, shards(): lax.all_to_all(whitened, 'chan', split_axis=3, concat_axis=2, tiled=True)  7.39 us
  transfers between devices with their start and end apart: 9, of which 9 were waited for; matrix products, arithmetic and copies ran while one was open for 10% of the time, Pallas kernels for 0%

commit v1 on v0

--- a/solution.py
+++ b/solution.py
@@ -1,7 +1,18 @@
+import functools
+
 import jax
 import jax.numpy as jnp
 from jax import lax
+from jax.experimental import pallas as pl
+from jax.experimental.pallas import tpu as pltpu
 from jax.sharding import PartitionSpec as P
+
+MESH = pl.DeviceIdType.MESH
+PLANES = 4
+SLOTS = 16
+
+UP = {0: [(0, 4), (4, 4), (8, 4)], 1: [(0, 4), (4, 4)], 2: [(2, 2), (4, 4)]}
+DOWN = {3: [(4, 4), (8, 4), (0, 4)], 2: [(4, 4), (8, 4)], 1: [(4, 4), (8, 2)]}
 
 
 def from_behind(block, axis, distance):
@@ -17,7 +28,7 @@
     return product / windows
 
 
-def shards(spectra, alive_mask):
+def ring_shards(spectra, alive_mask):
     channel_devices = lax.axis_size("chan")
     groups = spectra.shape[0]
     block_width = spectra.shape[3] // channel_devices
@@ -52,9 +63,237 @@
     return cross_band[None]
 
 
+def gather_kernel(x_hbm, alive_ref, h_ref, x_buf, g, load_sem, recv_z, recv_y, recv_c, send_z, send_y, send_c, out_sem):
+    me = lax.axis_index("chan")
+    z, y, c = me // 4, (me // 2) % 2, me % 2
+    y_peer = z * 4 + (1 - y) * 2 + c
+    c_peer = z * 4 + y * 2 + (1 - c)
+    width = x_buf.shape[1] // 16
+
+    loads = []
+    for f in range(2):
+        for part in range(2):
+            at = f * 2 + part
+            loads.append(pltpu.make_async_copy(x_hbm.at[f, part], x_buf.at[pl.ds(2 * at, 2)], load_sem.at[at]))
+    for load in loads:
+        load.start()
+
+    barrier = pltpu.get_barrier_semaphore()
+    pl.semaphore_signal(barrier, inc=1, device_id={"chan": y_peer}, device_id_type=MESH)
+    pl.semaphore_signal(barrier, inc=1, device_id={"chan": c_peer}, device_id_type=MESH)
+
+    @pl.when(z < PLANES - 1)
+    def _():
+        pl.semaphore_signal(barrier, inc=1, device_id={"chan": me + 4}, device_id_type=MESH)
+
+    @pl.when(z > 0)
+    def _():
+        pl.semaphore_signal(barrier, inc=1, device_id={"chan": me - 4}, device_id_type=MESH)
+
+    for load in loads:
+        load.wait()
+    for granule in range(8):
+        halves = []
+        for half in range(2):
+            at = pl.ds((2 * granule + half) * width, width)
+            x = x_buf[:, at]
+            square = x * x
+            row = lax.broadcasted_iota(jnp.int32, x.shape, 0)
+            is_real = (row // 2) % 2 == 0
+            other = jnp.where(is_real, pltpu.roll(square, 6, 0), pltpu.roll(square, 2, 0))
+            magnitude = jnp.sqrt(square + other)
+            factor = alive_ref[:, at].astype(jnp.float32) / jnp.maximum(magnitude, 1.0)
+            halves.append(x * factor)
+        tile = jnp.concatenate(halves, axis=0).astype(jnp.bfloat16)
+        g[me, granule] = tile
+        g[me, granule + 8] = tile
+
+    @pl.when((z == 0) | (z == PLANES - 1))
+    def _():
+        pl.semaphore_wait(barrier, 3)
+
+    @pl.when((z > 0) & (z < PLANES - 1))
+    def _():
+        pl.semaphore_wait(barrier, 4)
+
+    def remote(src, start, length, peer, send, recv):
+        view = g.at[src, pl.ds(start, length)]
+        return pltpu.make_async_remote_copy(
+            src_ref=view, dst_ref=view, send_sem=send, recv_sem=recv,
+            device_id={"chan": peer}, device_id_type=MESH,
+        )
+
+    def plane(zz):
+        base = (2 * zz + 4) % 8
+        column = lambda s: s * 4 + y * 2 + c
+        others = lambda s: s * 4 + (1 - y) * 2 + c
+        mine = base + y
+        sends = []
+        outs = []
+
+        def go(copy):
+            copy.start()
+            sends.append(copy)
+
+        def up(s, k):
+            start, length = UP[zz][k]
+            go(remote(column(s), start, length, me + 4, send_z.at[0, s, k], recv_z.at[s, k]))
+
+        def down(s, k):
+            start, length = DOWN[zz][k]
+            go(remote(column(s), start, length, me - 4, send_z.at[1, s, k], recv_z.at[s, k]))
+
+        def to_y(s):
+            go(remote(column(s), base + (1 - y), 5, y_peer, send_y.at[s], recv_y.at[s]))
+
+        def to_c(src, at):
+            go(remote(src, mine, 5, c_peer, send_c.at[at], recv_c.at[at]))
+
+        def keep(src, at):
+            copy = pltpu.make_async_copy(g.at[src, pl.ds(mine, 5)], h_ref.at[:, src], out_sem.at[at])
+            copy.start()
+            outs.append(copy)
+
+        def from_z(s):
+            windows = UP[zz - 1] if s < zz else DOWN[zz + 1]
+            for k, (start, length) in enumerate(windows):
+                remote(column(s), start, length, me, send_z.at[0, s, k], recv_z.at[s, k]).wait_recv()
+                if s < zz and zz < PLANES - 1 and k < len(UP[zz]):
+                    up(s, k)
+                if s > zz and zz > 0 and k < len(DOWN[zz]):
+                    down(s, k)
+            to_y(s)
+            to_c(column(s), s)
+            keep(column(s), s)
+
+        def from_y(s):
+            remote(others(s), mine, 5, me, send_y.at[s], recv_y.at[s]).wait_recv()
+            to_c(others(s), 4 + s)
+            keep(others(s), 4 + s)
+
+        def from_c(s, in_column):
+            src = s * 4 + (y if in_column else 1 - y) * 2 + (1 - c)
+            at = s if in_column else 4 + s
+            remote(src, mine, 5, me, send_c.at[at], recv_c.at[at]).wait_recv()
+            keep(src, 8 + at)
+
+        order = sorted((s for s in range(PLANES) if s != zz), key=lambda s: abs(s - zz))
+        for k in range(3):
+            if zz < PLANES - 1 and k < len(UP[zz]):
+                up(zz, k)
+            if zz > 0 and k < len(DOWN[zz]):
+                down(zz, k)
+        to_y(zz)
+        to_c(me, zz)
+        keep(me, zz)
+        from_z(order[0])
+        from_y(zz)
+        from_z(order[1])
+        from_y(order[0])
+        from_z(order[2])
+        from_y(order[1])
+        from_y(order[2])
+        from_c(zz, True)
+        from_c(order[0], True)
+        from_c(zz, False)
+        from_c(order[1], True)
+        from_c(order[0], False)
+        from_c(order[2], True)
+        from_c(order[1], False)
+        from_c(order[2], False)
+        for copy in sends:
+            copy.wait_send()
+        for copy in outs:
+            copy.wait()
+
+    for zz in range(PLANES):
+        pl.when(z == zz)(functools.partial(plane, zz))
+
+
+def gather(spectra, alive_mask):
+    width = spectra.shape[3] // 16
+    return pl.pallas_call(
+        gather_kernel,
+        out_shape=jax.ShapeDtypeStruct((5, 16, 16, width), jnp.bfloat16),
+        in_specs=[pl.BlockSpec(memory_space=pl.ANY), pl.BlockSpec(memory_space=pltpu.VMEM)],
+        out_specs=pl.BlockSpec(memory_space=pl.ANY),
+        scratch_shapes=[
+            pltpu.VMEM((8, 16 * width), jnp.float32),
+            pltpu.VMEM((16, SLOTS, 16, width), jnp.bfloat16),
+            pltpu.SemaphoreType.DMA((4,)),
+            pltpu.SemaphoreType.DMA((4, 3)),
+            pltpu.SemaphoreType.DMA((4,)),
+            pltpu.SemaphoreType.DMA((8,)),
+            pltpu.SemaphoreType.DMA((2, 4, 3)),
+            pltpu.SemaphoreType.DMA((4,)),
+            pltpu.SemaphoreType.DMA((8,)),
+            pltpu.SemaphoreType.DMA((16,)),
+        ],
+        compiler_params=pltpu.CompilerParams(
+            collective_id=0, has_side_effects=True, vmem_limit_bytes=24 * 2**20
+        ),
+        name="gather",
+    )(spectra, alive_mask.reshape(1, -1))
+
+
+def cross_kernel(scale, h_ref, out_ref, own, turned_rows):
+    step = pl.program_id(0)
+    c = lax.axis_index("chan") % 2
+    rows = h_ref.shape[1] * h_ref.shape[2]
+    width = h_ref.shape[3]
+
+    @pl.when(step == 0)
+    def _():
+        x = h_ref[4].reshape(rows, width).astype(jnp.float32)
+        row = lax.broadcasted_iota(jnp.int32, x.shape, 0)
+        block, group, part = (row // 8) % 2, (row // 4) % 2, (row // 2) % 2
+        swapped = jnp.where(block == 0, pltpu.roll(x, rows - 8, 0), pltpu.roll(x, 8, 0))
+        for t in range(2):
+            base = jnp.where(c == t, x, swapped)
+            turned = jnp.where(part == 0, pltpu.roll(base, rows - 2, 0), -pltpu.roll(base, 2, 0))
+            for f in range(2):
+                kept = (block == t) & (group == f)
+                own[t, f, :, pl.ds(0, width)] = jnp.where(kept, base, 0.0).astype(jnp.bfloat16)
+                own[t, f, :, pl.ds(width, width)] = jnp.where(kept, turned, 0.0).astype(jnp.bfloat16)
+        for q in range(5):
+            turned_rows[q] = h_ref[q].reshape(rows, width).T
+
+    place = 8 + c - step // 2
+    product = jnp.dot(
+        turned_rows[place // 2], own[place % 2, step % 2], preferred_element_type=jnp.float32
+    )
+    out_ref[0, 0] = product * scale
+
+
+def cross(gathered, windows):
+    width = gathered.shape[3]
+    return pl.pallas_call(
+        functools.partial(cross_kernel, 1.0 / windows),
+        out_shape=jax.ShapeDtypeStruct((9, 2, width, 2 * width), jnp.float32),
+        grid=(18,),
+        in_specs=[pl.BlockSpec(memory_space=pltpu.VMEM)],
+        out_specs=pl.BlockSpec((1, 1, width, 2 * width), lambda i: (i // 2, i % 2, 0, 0)),
+        scratch_shapes=[
+            pltpu.VMEM((2, 2, 256, 2 * width), jnp.bfloat16),
+            pltpu.VMEM((5, width, 256), jnp.bfloat16),
+        ],
+        compiler_params=pltpu.CompilerParams(vmem_limit_bytes=40 * 2**20),
+        name="cross",
+    )(gathered)
+
+
+def plane_shards(spectra, alive_mask):
+    gathered = gather(spectra, alive_mask)
+    return cross(gathered, 16 * spectra.shape[2])[None]
+
+
 def solution(mesh):
+    def local(spectra, alive_mask):
+        fits = lax.axis_size("chan") == 16 and spectra.shape == (2, 2, 2, 8192)
+        return (plane_shards if fits else ring_shards)(spectra, alive_mask)
+
     return jax.shard_map(
-        shards,
+        local,
         mesh=mesh,
         in_specs=(P("freq", None, "chan", None), P()),
         out_specs=P("chan", None, "freq", None, None),

time: 160 us -> 40.9 us (0.26)
  local copies, waits for them, and re-layouts: 77.9 us -> 1.71 us
  waiting for transfers between devices: 48.1 us -> 0 us
  Pallas kernels: 0 us -> 39 us
  matrix products: 22.8 us -> 0 us
  starting transfers between devices: 7.41 us -> 0 us
  other arithmetic: 3.06 us -> 0 us
    ppermute x8 -> x0, waiting for transfers between devices: 40.1 us -> none  [from_behind(): return lax.ppermute(block, axis, route)]
    pallas_call x0 -> x2, Pallas kernels: none -> 39 us  [the longest x1 21.5 us: gather(): pl.pallas_call(gather_kernel, out_shape=jax.ShapeDtypeStruct((5, 16, 16,...]
    unnamed x2 -> x4, local copies, waits for them, and re-layouts: 32.8 us -> 1.71 us
    dot_general x9 -> x0, matrix products: 22.8 us -> none  [cross_block(): jnp.einsum('fjw,fiw->fji', partner_block, own_stacked, preferred_element_...]
    all_to_all x1 -> x0, local copies, waits for them, and re-layouts: 19.2 us -> none  [shards(): lax.all_to_all(whitened, 'chan', split_axis=3, concat_axis=2, tiled=True)]
    convert_element_type x1 -> x0, local copies, waits for them, and re-layouts: 12.9 us -> none  [shards(): whitened = (spectra * factor[:, None]).astype(jnp.bfloat16)]
    dynamic_update_slice x1 -> x0, local copies, waits for them, and re-layouts: 12.9 us -> none  [shards(): lax.dynamic_update_index_in_dim(empty_band, cross_block(own_stacked, own_...]
    all_to_all x1 -> x0, waiting for transfers between devices: 7.94 us -> none  [shards(): lax.all_to_all(whitened, 'chan', split_axis=3, concat_axis=2, tiled=True)]
  transfers between devices with their start and end apart: 9 -> 0, of which waited for: 9 -> 0; matrix products, arithmetic and copies ran while one was open for 10% -> 0% of each run, Pallas kernels for 0% -> 0%
where the time goes in v1:
time: 40.9 us; the launch traced here: 40.7 us
  Pallas kernels  39 us (95%)
  local copies, waits for them, and re-layouts  1.71 us (4%)
    pallas_call x1, Pallas kernels, gather(): pl.pallas_call(gather_kernel, out_shape=jax.ShapeDtypeStruct((5, 16, 16,...  21.5 us
    pallas_call x1, Pallas kernels, cross(): pl.pallas_call(functools.partial(cross_kernel, 1.0 / windows), out_shape=...  17.5 us
    unnamed x4, local copies, waits for them, and re-layouts  1.71 us

profile of v1, /device:TPU:0, one launch (start us, length us, event | category | flops | bytes accessed | tf_op | source)
XLA Modules:
  0.0 40.7 jit_solution(12614351316916571671)
XLA Ops:
  0.0 0.0 copy-start
  0.0 0.9 %copy-done = f32[2,2,2,8192]{3,2,1,0:T(2,128)S(1)} copy-done((f32[2,2,2,8192]{3,2,1,0:T(2,128)S(1)}, f32[2,2,2,8192]{3,2,1,0:T(2,128)}, u32[]{:S(2)}) %copy-start) | copy-done | bytes 262168
  1.0 0.0 copy-start.1
  1.0 0.8 %copy-done.1 = s32[8192]{0:T(1024)S(1)} copy-done((s32[8192]{0:T(1024)S(1)}, s32[8192]{0:T(1024)}, u32[]{:S(2)}) %copy-start.1) | copy-done | bytes 32792
  1.7 21.5 %gather.1.h_ref = bf16[5,16,16,512]{3,2,1,0:T(8,128)(2,1)S(1)} custom-call(f32[2,2,2,8192]{3,2,1,0:T(2,128)S(1)} %copy-done, s32[1,8192]{1,0:T(1,128)S(1)} %bitcast.2), custom_call_target="tpu_custom_call" | custom-call | tf_op jit(solution)/shard_map/gather/pallas_call | solution.py:215
  23.2 17.5 %cross.1 = f32[9,2,512,1024]{3,2,1,0:T(8,128)} custom-call(bf16[5,16,16,512]{3,2,1,0:T(8,128)(2,1)S(1)} %gather.1.h_ref), custom_call_target="tpu_custom_call" | custom-call | tf_op jit(solution)/shard_map/cross/pallas_call | solution.py:270
Async XLA Ops:
  0.0 0.9 %copy-start = (f32[2,2,2,8192]{3,2,1,0:T(2,128)S(1)}, f32[2,2,2,8192]{3,2,1,0:T(2,128)}, u32[]{:S(2)}) copy-start(f32[2,2,2,8192]{3,2,1,0:T(2,128)} %x_hbm.1) | copy-start | bytes 786436
  1.0 0.8 %copy-start.1 = (s32[8192]{0:T(1024)S(1)}, s32[8192]{0:T(1024)}, u32[]{:S(2)}) copy-start(s32[8192]{0:T(1024)} %param.3) | copy-start | bytes 98308

commit v2 on v1

--- a/solution.py
+++ b/solution.py
@@ -10,6 +10,9 @@
 MESH = pl.DeviceIdType.MESH
 PLANES = 4
 SLOTS = 16
+LAGS = 9
+DEPTH = 4
+HALVES = 2
 
 UP = {0: [(0, 4), (4, 4), (8, 4)], 1: [(0, 4), (4, 4)], 2: [(2, 2), (4, 4)]}
 DOWN = {3: [(4, 4), (8, 4), (0, 4)], 2: [(4, 4), (8, 4)], 1: [(4, 4), (8, 2)]}
@@ -63,7 +66,7 @@
     return cross_band[None]
 
 
-def gather_kernel(x_hbm, alive_ref, h_ref, x_buf, g, load_sem, recv_z, recv_y, recv_c, send_z, send_y, send_c, out_sem):
+def gather_kernel(x_hbm, alive_hbm, h_ref, x_buf, alive_ref, g, load_sem, recv_z, recv_y, recv_c, send_z, send_y, send_c, out_sem):
     me = lax.axis_index("chan")
     z, y, c = me // 4, (me // 2) % 2, me % 2
     y_peer = z * 4 + (1 - y) * 2 + c
@@ -75,6 +78,7 @@
         for part in range(2):
             at = f * 2 + part
             loads.append(pltpu.make_async_copy(x_hbm.at[f, part], x_buf.at[pl.ds(2 * at, 2)], load_sem.at[at]))
+    loads.append(pltpu.make_async_copy(alive_hbm, alive_ref, load_sem.at[4]))
     for load in loads:
         load.start()
 
@@ -215,12 +219,13 @@
     return pl.pallas_call(
         gather_kernel,
         out_shape=jax.ShapeDtypeStruct((5, 16, 16, width), jnp.bfloat16),
-        in_specs=[pl.BlockSpec(memory_space=pl.ANY), pl.BlockSpec(memory_space=pltpu.VMEM)],
+        in_specs=[pl.BlockSpec(memory_space=pltpu.HBM)] * 2,
         out_specs=pl.BlockSpec(memory_space=pl.ANY),
         scratch_shapes=[
             pltpu.VMEM((8, 16 * width), jnp.float32),
+            pltpu.VMEM((1, 16 * width), jnp.int32),
             pltpu.VMEM((16, SLOTS, 16, width), jnp.bfloat16),
-            pltpu.SemaphoreType.DMA((4,)),
+            pltpu.SemaphoreType.DMA((5,)),
             pltpu.SemaphoreType.DMA((4, 3)),
             pltpu.SemaphoreType.DMA((4,)),
             pltpu.SemaphoreType.DMA((8,)),
@@ -233,51 +238,81 @@
             collective_id=0, has_side_effects=True, vmem_limit_bytes=24 * 2**20
         ),
         name="gather",
-    )(spectra, alive_mask.reshape(1, -1))
-
-
-def cross_kernel(scale, h_ref, out_ref, own, turned_rows):
-    step = pl.program_id(0)
+    )(
+        pltpu.with_memory_space_constraint(spectra, pltpu.HBM),
+        pltpu.with_memory_space_constraint(alive_mask.reshape(1, -1), pltpu.HBM),
+    )
+
+
+def cross_kernel(scale, h_ref, out_ref, own, partner, ring, sems):
     c = lax.axis_index("chan") % 2
     rows = h_ref.shape[1] * h_ref.shape[2]
     width = h_ref.shape[3]
-
-    @pl.when(step == 0)
-    def _():
-        x = h_ref[4].reshape(rows, width).astype(jnp.float32)
-        row = lax.broadcasted_iota(jnp.int32, x.shape, 0)
-        block, group, part = (row // 8) % 2, (row // 4) % 2, (row // 2) % 2
-        swapped = jnp.where(block == 0, pltpu.roll(x, rows - 8, 0), pltpu.roll(x, 8, 0))
-        for t in range(2):
-            base = jnp.where(c == t, x, swapped)
+    half = width // HALVES
+
+    def out_copy(lag, f, piece):
+        slot = lag % DEPTH
+        return pltpu.make_async_copy(
+            ring.at[slot, f, pl.ds(piece * half, half)],
+            out_ref.at[lag, f, pl.ds(piece * half, half)],
+            sems.at[slot, f, piece],
+        )
+
+    def one_lag(lag, _):
+        place = 8 + c - lag
+        kind = place % 2
+
+        @pl.when(lag < 2)
+        def _():
+            x = h_ref[4].reshape(rows, width).astype(jnp.float32)
+            row = lax.broadcasted_iota(jnp.int32, x.shape, 0)
+            block, group, part = (row // 8) % 2, (row // 4) % 2, (row // 2) % 2
+            swapped = jnp.where(block == 0, pltpu.roll(x, rows - 8, 0), pltpu.roll(x, 8, 0))
+            base = jnp.where(lag == 0, x, swapped)
             turned = jnp.where(part == 0, pltpu.roll(base, rows - 2, 0), -pltpu.roll(base, 2, 0))
             for f in range(2):
-                kept = (block == t) & (group == f)
-                own[t, f, :, pl.ds(0, width)] = jnp.where(kept, base, 0.0).astype(jnp.bfloat16)
-                own[t, f, :, pl.ds(width, width)] = jnp.where(kept, turned, 0.0).astype(jnp.bfloat16)
-        for q in range(5):
-            turned_rows[q] = h_ref[q].reshape(rows, width).T
-
-    place = 8 + c - step // 2
-    product = jnp.dot(
-        turned_rows[place // 2], own[place % 2, step % 2], preferred_element_type=jnp.float32
-    )
-    out_ref[0, 0] = product * scale
+                kept = (block == kind) & (group == f)
+                own[kind, f, :, pl.ds(0, width)] = jnp.where(kept, base, 0.0).astype(jnp.bfloat16)
+                own[kind, f, :, pl.ds(width, width)] = jnp.where(kept, turned, 0.0).astype(jnp.bfloat16)
+
+        @pl.when((lag == 0) | (kind == 1))
+        def _():
+            partner[...] = h_ref[place // 2].reshape(rows, width).T
+
+        for f in range(2):
+            for piece in range(HALVES):
+                at = pl.ds(piece * half, half)
+                product = jnp.dot(partner[at, :], own[kind, f], preferred_element_type=jnp.float32)
+
+                @pl.when(lag >= DEPTH)
+                def _():
+                    out_copy(lag - DEPTH, f, piece).wait()
+
+                ring[lag % DEPTH, f, at] = product * scale
+                out_copy(lag, f, piece).start()
+        return 0
+
+    lax.fori_loop(0, LAGS, one_lag, 0)
+    for lag in range(LAGS - DEPTH, LAGS):
+        for f in range(2):
+            for piece in range(HALVES):
+                out_copy(lag, f, piece).wait()
 
 
 def cross(gathered, windows):
     width = gathered.shape[3]
     return pl.pallas_call(
         functools.partial(cross_kernel, 1.0 / windows),
-        out_shape=jax.ShapeDtypeStruct((9, 2, width, 2 * width), jnp.float32),
-        grid=(18,),
+        out_shape=jax.ShapeDtypeStruct((LAGS, 2, width, 2 * width), jnp.float32),
         in_specs=[pl.BlockSpec(memory_space=pltpu.VMEM)],
-        out_specs=pl.BlockSpec((1, 1, width, 2 * width), lambda i: (i // 2, i % 2, 0, 0)),
+        out_specs=pl.BlockSpec(memory_space=pltpu.HBM),
         scratch_shapes=[
             pltpu.VMEM((2, 2, 256, 2 * width), jnp.bfloat16),
-            pltpu.VMEM((5, width, 256), jnp.bfloat16),
+            pltpu.VMEM((width, 256), jnp.bfloat16),
+            pltpu.VMEM((DEPTH, 2, width, 2 * width), jnp.float32),
+            pltpu.SemaphoreType.DMA((DEPTH, 2, HALVES)),
         ],
-        compiler_params=pltpu.CompilerParams(vmem_limit_bytes=40 * 2**20),
+        compiler_params=pltpu.CompilerParams(vmem_limit_bytes=28 * 2**20),
         name="cross",
     )(gathered)
 

time: 40.9 us -> 36.5 us (0.89)
  Pallas kernels: 39 us -> 36.3 us
  local copies, waits for them, and re-layouts: 1.71 us -> 0 us
    pallas_call x1, Pallas kernels: 17.5 us -> 14.9 us  [cross(): pl.pallas_call(functools.partial(cross_kernel, 1.0 / windows), out_shape=...]
    unnamed x4 -> x0, local copies, waits for them, and re-layouts: 1.71 us -> none
where the time goes in v2:
time: 36.5 us; the launch traced here: 36.3 us
  Pallas kernels  36.3 us (99%)
    pallas_call x1, Pallas kernels, gather(): pl.pallas_call(gather_kernel, out_shape=jax.ShapeDtypeStruct((5, 16, 16,...  21.4 us
    pallas_call x1, Pallas kernels, cross(): pl.pallas_call(functools.partial(cross_kernel, 1.0 / windows), out_shape=...  14.9 us

profile of v2, /device:TPU:0, one launch (start us, length us, event | category | flops | bytes accessed | tf_op | source)
XLA Modules:
  0.0 36.3 jit_solution(12940952308275174735)
XLA Ops:
  0.0 21.4 %gather.1.h_ref = bf16[5,16,16,512]{3,2,1,0:T(8,128)(2,1)S(1)} custom-call(f32[2,2,2,8192]{3,2,1,0:T(2,128)} %x_hbm.1, s32[1,8192]{1,0:T(1,128)} %bitcast.2), custom_call_target="tpu_custom_call" | custom-call | tf_op jit(solution)/shard_map/gather/pallas_call | solution.py:219
  21.4 14.9 %cross.1 = f32[9,2,512,1024]{3,2,1,0:T(8,128)} custom-call(bf16[5,16,16,512]{3,2,1,0:T(8,128)(2,1)S(1)} %gather.1.h_ref), custom_call_target="tpu_custom_call" | custom-call | tf_op jit(solution)/shard_map/cross/pallas_call | solution.py:304

commit v3 on v2

--- a/solution.py
+++ b/solution.py
@@ -14,8 +14,8 @@
 DEPTH = 4
 HALVES = 2
 
-UP = {0: [(0, 4), (4, 4), (8, 4)], 1: [(0, 4), (4, 4)], 2: [(2, 2), (4, 4)]}
-DOWN = {3: [(4, 4), (8, 4), (0, 4)], 2: [(4, 4), (8, 4)], 1: [(4, 4), (8, 2)]}
+PIECES = [(0, 3), (3, 3)]
+NEED = 6
 
 
 def from_behind(block, axis, distance):
@@ -86,13 +86,8 @@
     pl.semaphore_signal(barrier, inc=1, device_id={"chan": y_peer}, device_id_type=MESH)
     pl.semaphore_signal(barrier, inc=1, device_id={"chan": c_peer}, device_id_type=MESH)
 
-    @pl.when(z < PLANES - 1)
-    def _():
-        pl.semaphore_signal(barrier, inc=1, device_id={"chan": me + 4}, device_id_type=MESH)
-
-    @pl.when(z > 0)
-    def _():
-        pl.semaphore_signal(barrier, inc=1, device_id={"chan": me - 4}, device_id_type=MESH)
+    for hop in range(1, PLANES):
+        pl.semaphore_signal(barrier, inc=1, device_id={"chan": (me + 4 * hop) % 16}, device_id_type=MESH)
 
     for load in loads:
         load.wait()
@@ -109,130 +104,123 @@
             factor = alive_ref[:, at].astype(jnp.float32) / jnp.maximum(magnitude, 1.0)
             halves.append(x * factor)
         tile = jnp.concatenate(halves, axis=0).astype(jnp.bfloat16)
-        g[me, granule] = tile
-        g[me, granule + 8] = tile
-
-    @pl.when((z == 0) | (z == PLANES - 1))
-    def _():
-        pl.semaphore_wait(barrier, 3)
-
-    @pl.when((z > 0) & (z < PLANES - 1))
-    def _():
-        pl.semaphore_wait(barrier, 4)
-
-    def remote(src, start, length, peer, send, recv):
-        view = g.at[src, pl.ds(start, length)]
-        return pltpu.make_async_remote_copy(
-            src_ref=view, dst_ref=view, send_sem=send, recv_sem=recv,
-            device_id={"chan": peer}, device_id_type=MESH,
-        )
-
-    def plane(zz):
-        base = (2 * zz + 4) % 8
-        column = lambda s: s * 4 + y * 2 + c
-        others = lambda s: s * 4 + (1 - y) * 2 + c
-        mine = base + y
+        g[granule] = tile
+        g[granule + 8] = tile
+
+    pl.semaphore_wait(barrier, 5)
+
+    def chip(zz, yy):
+        first = lambda plane: (2 * plane + 4) % 8
+        column = lambda s: s * 4 + yy * 2 + c
+        others = lambda s: s * 4 + (1 - yy) * 2 + c
         sends = []
-        outs = []
+
+        def remote(view, src, start, length, peer, send, recv):
+            return pltpu.make_async_remote_copy(
+                src_ref=view, dst_ref=h_ref.at[pl.ds(start, length), src], send_sem=send, recv_sem=recv,
+                device_id={"chan": peer}, device_id_type=MESH,
+            )
 
         def go(copy):
             copy.start()
             sends.append(copy)
 
-        def up(s, k):
-            start, length = UP[zz][k]
-            go(remote(column(s), start, length, me + 4, send_z.at[0, s, k], recv_z.at[s, k]))
-
-        def down(s, k):
-            start, length = DOWN[zz][k]
-            go(remote(column(s), start, length, me - 4, send_z.at[1, s, k], recv_z.at[s, k]))
-
-        def to_y(s):
-            go(remote(column(s), base + (1 - y), 5, y_peer, send_y.at[s], recv_y.at[s]))
-
-        def to_c(src, at):
-            go(remote(src, mine, 5, c_peer, send_c.at[at], recv_c.at[at]))
-
-        def keep(src, at):
-            copy = pltpu.make_async_copy(g.at[src, pl.ds(mine, 5)], h_ref.at[:, src], out_sem.at[at])
-            copy.start()
-            outs.append(copy)
-
-        def from_z(s):
-            windows = UP[zz - 1] if s < zz else DOWN[zz + 1]
-            for k, (start, length) in enumerate(windows):
-                remote(column(s), start, length, me, send_z.at[0, s, k], recv_z.at[s, k]).wait_recv()
-                if s < zz and zz < PLANES - 1 and k < len(UP[zz]):
-                    up(s, k)
-                if s > zz and zz > 0 and k < len(DOWN[zz]):
-                    down(s, k)
-            to_y(s)
-            to_c(column(s), s)
-            keep(column(s), s)
-
-        def from_y(s):
-            remote(others(s), mine, 5, me, send_y.at[s], recv_y.at[s]).wait_recv()
-            to_c(others(s), 4 + s)
-            keep(others(s), 4 + s)
-
-        def from_c(s, in_column):
-            src = s * 4 + (y if in_column else 1 - y) * 2 + (1 - c)
-            at = s if in_column else 4 + s
-            remote(src, mine, 5, me, send_c.at[at], recv_c.at[at]).wait_recv()
-            keep(src, 8 + at)
+        def cut(k, chip_y):
+            start, length = PIECES[k]
+            low, high = max(start, chip_y), min(start + length, chip_y + 5)
+            return low, high - low
+
+        def view_of(s, start, length):
+            if s == zz:
+                return g.at[pl.ds(first(zz) + start, length)]
+            return h_ref.at[pl.ds(start, length), column(s)]
+
+        def to_z(s, k):
+            start, length = PIECES[k]
+            view = g.at[pl.ds(first(s) + start, length)]
+            go(remote(view, me, start, length, s * 4 + yy * 2 + c, send_z.at[s, k], recv_z.at[zz, k]))
+
+        def to_y(s, k):
+            start, length = cut(k, 1 - yy)
+            go(remote(view_of(s, start, length), column(s), start, length, y_peer, send_y.at[s, k], recv_y.at[s, k]))
+
+        def to_c(s, k, in_column):
+            start, length = cut(k, yy)
+            src = column(s) if in_column else others(s)
+            view = view_of(s, start, length) if in_column else h_ref.at[pl.ds(start, length), src]
+            at = s if in_column else PLANES + s
+            go(remote(view, src, start, length, c_peer, send_c.at[at, k], recv_c.at[at, k]))
+
+        def from_z(s, k):
+            start, length = PIECES[k]
+            view = g.at[pl.ds(start, length)]
+            remote(view, column(s), start, length, y_peer, send_z.at[s, k], recv_z.at[s, k]).wait_recv()
+            to_y(s, k)
+            to_c(s, k, True)
+
+        def from_y(s, k):
+            start, length = cut(k, yy)
+            view = g.at[pl.ds(start, length)]
+            remote(view, others(s), start, length, y_peer, send_y.at[s, k], recv_y.at[s, k]).wait_recv()
+            to_c(s, k, False)
+
+        def from_c(s, k, in_column):
+            start, length = cut(k, yy)
+            src = s * 4 + (yy if in_column else 1 - yy) * 2 + (1 - c)
+            at = s if in_column else PLANES + s
+            view = g.at[pl.ds(start, length)]
+            remote(view, src, start, length, c_peer, send_c.at[at, k], recv_c.at[at, k]).wait_recv()
 
         order = sorted((s for s in range(PLANES) if s != zz), key=lambda s: abs(s - zz))
-        for k in range(3):
-            if zz < PLANES - 1 and k < len(UP[zz]):
-                up(zz, k)
-            if zz > 0 and k < len(DOWN[zz]):
-                down(zz, k)
-        to_y(zz)
-        to_c(me, zz)
-        keep(me, zz)
-        from_z(order[0])
-        from_y(zz)
-        from_z(order[1])
-        from_y(order[0])
-        from_z(order[2])
-        from_y(order[1])
-        from_y(order[2])
-        from_c(zz, True)
-        from_c(order[0], True)
-        from_c(zz, False)
-        from_c(order[1], True)
-        from_c(order[0], False)
-        from_c(order[2], True)
-        from_c(order[1], False)
-        from_c(order[2], False)
+        count = len(PIECES)
+        for k in range(count):
+            for s in reversed(order):
+                to_z(s, k)
+            to_y(zz, k)
+        for k in range(count):
+            to_c(zz, k, True)
+        keep = pltpu.make_async_copy(g.at[pl.ds(first(zz), NEED)], h_ref.at[:, me], out_sem)
+        keep.start()
+        for k in range(count):
+            from_y(zz, k)
+            for s in order:
+                from_z(s, k)
+                if k > 0:
+                    from_y(s, k - 1)
+        for s in order:
+            from_y(s, count - 1)
+        for k in range(count):
+            for in_column in (True, False):
+                for s in [zz] + order:
+                    from_c(s, k, in_column)
         for copy in sends:
             copy.wait_send()
-        for copy in outs:
-            copy.wait()
+        keep.wait()
 
     for zz in range(PLANES):
-        pl.when(z == zz)(functools.partial(plane, zz))
+        for yy in range(2):
+            pl.when((z == zz) & (y == yy))(functools.partial(chip, zz, yy))
 
 
 def gather(spectra, alive_mask):
     width = spectra.shape[3] // 16
     return pl.pallas_call(
         gather_kernel,
-        out_shape=jax.ShapeDtypeStruct((5, 16, 16, width), jnp.bfloat16),
+        out_shape=jax.ShapeDtypeStruct((NEED, 16, 16, width), jnp.bfloat16),
         in_specs=[pl.BlockSpec(memory_space=pltpu.HBM)] * 2,
         out_specs=pl.BlockSpec(memory_space=pl.ANY),
         scratch_shapes=[
             pltpu.VMEM((8, 16 * width), jnp.float32),
             pltpu.VMEM((1, 16 * width), jnp.int32),
-            pltpu.VMEM((16, SLOTS, 16, width), jnp.bfloat16),
+            pltpu.VMEM((SLOTS, 16, width), jnp.bfloat16),
             pltpu.SemaphoreType.DMA((5,)),
-            pltpu.SemaphoreType.DMA((4, 3)),
-            pltpu.SemaphoreType.DMA((4,)),
-            pltpu.SemaphoreType.DMA((8,)),
-            pltpu.SemaphoreType.DMA((2, 4, 3)),
-            pltpu.SemaphoreType.DMA((4,)),
-            pltpu.SemaphoreType.DMA((8,)),
-            pltpu.SemaphoreType.DMA((16,)),
+            pltpu.SemaphoreType.DMA((4, len(PIECES))),
+            pltpu.SemaphoreType.DMA((4, len(PIECES))),
+            pltpu.SemaphoreType.DMA((8, len(PIECES))),
+            pltpu.SemaphoreType.DMA((4, len(PIECES))),
+            pltpu.SemaphoreType.DMA((4, len(PIECES))),
+            pltpu.SemaphoreType.DMA((8, len(PIECES))),
+            pltpu.SemaphoreType.DMA,
         ],
         compiler_params=pltpu.CompilerParams(
             collective_id=0, has_side_effects=True, vmem_limit_bytes=24 * 2**20
@@ -245,7 +233,8 @@
 
 
 def cross_kernel(scale, h_ref, out_ref, own, partner, ring, sems):
-    c = lax.axis_index("chan") % 2
+    me = lax.axis_index("chan")
+    y, c = (me // 2) % 2, me % 2
     rows = h_ref.shape[1] * h_ref.shape[2]
     width = h_ref.shape[3]
     half = width // HALVES
@@ -264,7 +253,7 @@
 
         @pl.when(lag < 2)
         def _():
-            x = h_ref[4].reshape(rows, width).astype(jnp.float32)
+            x = h_ref[4 + y].reshape(rows, width).astype(jnp.float32)
             row = lax.broadcasted_iota(jnp.int32, x.shape, 0)
             block, group, part = (row // 8) % 2, (row // 4) % 2, (row // 2) % 2
             swapped = jnp.where(block == 0, pltpu.roll(x, rows - 8, 0), pltpu.roll(x, 8, 0))
@@ -277,7 +266,7 @@
 
         @pl.when((lag == 0) | (kind == 1))
         def _():
-            partner[...] = h_ref[place // 2].reshape(rows, width).T
+            partner[...] = h_ref[y + place // 2].reshape(rows, width).T
 
         for f in range(2):
             for piece in range(HALVES):

time: 36.5 us -> 35.1 us (0.962)
  the two profiles are of different devices: /device:TPU:0 before, /device:TPU:21 now
where the time goes in v3:
time: 35.1 us; the launch traced here: 35 us
  Pallas kernels  35 us (100%)
    pallas_call x1, Pallas kernels, gather(): pl.pallas_call(gather_kernel, out_shape=jax.ShapeDtypeStruct((NEED, 16, 1...  20 us
    pallas_call x1, Pallas kernels, cross(): pl.pallas_call(functools.partial(cross_kernel, 1.0 / windows), out_shape=...  14.9 us

profile of v3, /device:TPU:21, one launch (start us, length us, event | category | flops | bytes accessed | tf_op | source)
XLA Modules:
  0.0 35.0 jit_solution(8972618194825241121)
XLA Ops:
  0.0 20.0 %gather.1.h_ref = bf16[6,16,16,512]{3,2,1,0:T(8,128)(2,1)S(1)} custom-call(f32[2,2,2,8192]{3,2,1,0:T(2,128)} %x_hbm.1, s32[1,8192]{1,0:T(1,128)} %bitcast.2), custom_call_target="tpu_custom_call" | custom-call | tf_op jit(solution)/shard_map/gather/pallas_call | solution.py:207
  20.0 14.9 %cross.1 = f32[9,2,512,1024]{3,2,1,0:T(8,128)} custom-call(bf16[6,16,16,512]{3,2,1,0:T(8,128)(2,1)S(1)} %gather.1.h_ref), custom_call_target="tpu_custom_call" | custom-call | tf_op jit(solution)/shard_map/cross/pallas_call | solution.py:293

commit v4 on v3

--- a/solution.py
+++ b/solution.py
@@ -12,10 +12,17 @@
 SLOTS = 16
 LAGS = 9
 DEPTH = 4
-HALVES = 2
-
-PIECES = [(0, 3), (3, 3)]
+HALVES = 1
+
+PIECES = [
+    [(2, 3), (0, 2), (5, 1)],
+    [(0, 3), (3, 3)],
+    [(3, 3), (0, 3)],
+    [(1, 3), (4, 2), (0, 1)],
+]
+MAX_PIECES = 3
 NEED = 6
+PASSED = {(2, 0): 3, (2, 1): 3, (1, 3): 0, (1, 2): 0}
 
 
 def from_behind(block, axis, distance):
@@ -66,7 +73,7 @@
     return cross_band[None]
 
 
-def gather_kernel(x_hbm, alive_hbm, h_ref, x_buf, alive_ref, g, load_sem, recv_z, recv_y, recv_c, send_z, send_y, send_c, out_sem):
+def gather_kernel(x_hbm, alive_hbm, h_ref, x_buf, alive_ref, g, load_sem, recv_z, recv_y, recv_c, send_z, send_y, send_c, send_p, out_sem):
     me = lax.axis_index("chan")
     z, y, c = me // 4, (me // 2) % 2, me % 2
     y_peer = z * 4 + (1 - y) * 2 + c
@@ -126,9 +133,9 @@
             sends.append(copy)
 
         def cut(k, chip_y):
-            start, length = PIECES[k]
+            start, length = PIECES[zz][k]
             low, high = max(start, chip_y), min(start + length, chip_y + 5)
-            return low, high - low
+            return low, max(high - low, 0)
 
         def view_of(s, start, length):
             if s == zz:
@@ -136,59 +143,75 @@
             return h_ref.at[pl.ds(start, length), column(s)]
 
         def to_z(s, k):
-            start, length = PIECES[k]
+            if k >= len(PIECES[s]) or (k == 0 and s in (PASSED.get((2, zz)), PASSED.get((1, zz)))):
+                return
+            start, length = PIECES[s][k]
             view = g.at[pl.ds(first(s) + start, length)]
             go(remote(view, me, start, length, s * 4 + yy * 2 + c, send_z.at[s, k], recv_z.at[zz, k]))
 
         def to_y(s, k):
             start, length = cut(k, 1 - yy)
+            if not length:
+                return
             go(remote(view_of(s, start, length), column(s), start, length, y_peer, send_y.at[s, k], recv_y.at[s, k]))
 
         def to_c(s, k, in_column):
             start, length = cut(k, yy)
+            if not length:
+                return
             src = column(s) if in_column else others(s)
             view = view_of(s, start, length) if in_column else h_ref.at[pl.ds(start, length), src]
             at = s if in_column else PLANES + s
             go(remote(view, src, start, length, c_peer, send_c.at[at, k], recv_c.at[at, k]))
 
         def from_z(s, k):
-            start, length = PIECES[k]
+            start, length = PIECES[zz][k]
             view = g.at[pl.ds(start, length)]
             remote(view, column(s), start, length, y_peer, send_z.at[s, k], recv_z.at[s, k]).wait_recv()
+            if k == 0 and (zz, s) in PASSED:
+                to = PASSED[zz, s]
+                view = h_ref.at[pl.ds(start, length), column(s)]
+                peer = to * 4 + yy * 2 + c
+                go(remote(view, column(s), PIECES[to][0][0], length, peer, send_p.at[s], recv_z.at[s, 0]))
             to_y(s, k)
             to_c(s, k, True)
 
         def from_y(s, k):
             start, length = cut(k, yy)
+            if not length:
+                return
             view = g.at[pl.ds(start, length)]
             remote(view, others(s), start, length, y_peer, send_y.at[s, k], recv_y.at[s, k]).wait_recv()
             to_c(s, k, False)
 
         def from_c(s, k, in_column):
             start, length = cut(k, yy)
+            if not length:
+                return
             src = s * 4 + (yy if in_column else 1 - yy) * 2 + (1 - c)
             at = s if in_column else PLANES + s
             view = g.at[pl.ds(start, length)]
             remote(view, src, start, length, c_peer, send_c.at[at, k], recv_c.at[at, k]).wait_recv()
 
         order = sorted((s for s in range(PLANES) if s != zz), key=lambda s: abs(s - zz))
-        count = len(PIECES)
+        count = len(PIECES[zz])
         for k in range(count):
-            for s in reversed(order):
+            to_y(zz, k)
+        for s in order:
+            for k in range(MAX_PIECES):
                 to_z(s, k)
-            to_y(zz, k)
         for k in range(count):
             to_c(zz, k, True)
         keep = pltpu.make_async_copy(g.at[pl.ds(first(zz), NEED)], h_ref.at[:, me], out_sem)
         keep.start()
         for k in range(count):
             from_y(zz, k)
-            for s in order:
+        for s in order:
+            for k in range(count):
                 from_z(s, k)
-                if k > 0:
-                    from_y(s, k - 1)
         for s in order:
-            from_y(s, count - 1)
+            for k in range(count):
+                from_y(s, k)
         for k in range(count):
             for in_column in (True, False):
                 for s in [zz] + order:
@@ -214,12 +237,13 @@
             pltpu.VMEM((1, 16 * width), jnp.int32),
             pltpu.VMEM((SLOTS, 16, width), jnp.bfloat16),
             pltpu.SemaphoreType.DMA((5,)),
-            pltpu.SemaphoreType.DMA((4, len(PIECES))),
-            pltpu.SemaphoreType.DMA((4, len(PIECES))),
-            pltpu.SemaphoreType.DMA((8, len(PIECES))),
-            pltpu.SemaphoreType.DMA((4, len(PIECES))),
-            pltpu.SemaphoreType.DMA((4, len(PIECES))),
-            pltpu.SemaphoreType.DMA((8, len(PIECES))),
+            pltpu.SemaphoreType.DMA((4, MAX_PIECES)),
+            pltpu.SemaphoreType.DMA((4, MAX_PIECES)),
+            pltpu.SemaphoreType.DMA((8, MAX_PIECES)),
+            pltpu.SemaphoreType.DMA((4, MAX_PIECES)),
+            pltpu.SemaphoreType.DMA((4, MAX_PIECES)),
+            pltpu.SemaphoreType.DMA((8, MAX_PIECES)),
+            pltpu.SemaphoreType.DMA((4,)),
             pltpu.SemaphoreType.DMA,
         ],
         compiler_params=pltpu.CompilerParams(

time: 35.1 us -> 33.6 us (0.957)
  the two profiles are of different devices: /device:TPU:21 before, /device:TPU:0 now
where the time goes in v4:
time: 33.6 us; the launch traced here: 33.4 us
  Pallas kernels  33.4 us (99%)
    pallas_call x1, Pallas kernels, gather(): pl.pallas_call(gather_kernel, out_shape=jax.ShapeDtypeStruct((NEED, 16, 1...  19.5 us
    pallas_call x1, Pallas kernels, cross(): pl.pallas_call(functools.partial(cross_kernel, 1.0 / windows), out_shape=...  13.9 us

profile of v4, /device:TPU:0, one launch (start us, length us, event | category | flops | bytes accessed | tf_op | source)
XLA Modules:
  0.0 33.4 jit_solution(5728587258412271574)
XLA Ops:
  0.0 19.5 %gather.1.h_ref = bf16[6,16,16,512]{3,2,1,0:T(8,128)(2,1)S(1)} custom-call(f32[2,2,2,8192]{3,2,1,0:T(2,128)} %x_hbm.1, s32[1,8192]{1,0:T(1,128)} %bitcast.2), custom_call_target="tpu_custom_call" | custom-call | tf_op jit(solution)/shard_map/gather/pallas_call | solution.py:230
  19.5 13.9 %cross.1 = f32[9,2,512,1024]{3,2,1,0:T(8,128)} custom-call(bf16[6,16,16,512]{3,2,1,0:T(8,128)(2,1)S(1)} %gather.1.h_ref), custom_call_target="tpu_custom_call" | custom-call | tf_op jit(solution)/shard_map/cross/pallas_call | solution.py:317

commit v5 on v4

--- a/solution.py
+++ b/solution.py
@@ -195,19 +195,25 @@
 
         order = sorted((s for s in range(PLANES) if s != zz), key=lambda s: abs(s - zz))
         count = len(PIECES[zz])
+        urgent = [s for s in order if (s, zz) in PASSED]
+        for s in urgent:
+            to_z(s, 0)
         for k in range(count):
             to_y(zz, k)
         for s in order:
-            for k in range(MAX_PIECES):
+            for k in range(1 if s in urgent else 0, MAX_PIECES):
                 to_z(s, k)
         for k in range(count):
             to_c(zz, k, True)
         keep = pltpu.make_async_copy(g.at[pl.ds(first(zz), NEED)], h_ref.at[:, me], out_sem)
         keep.start()
+        passing = [s for s in order if (zz, s) in PASSED]
+        for s in passing:
+            from_z(s, 0)
         for k in range(count):
             from_y(zz, k)
         for s in order:
-            for k in range(count):
+            for k in range(1 if s in passing else 0, count):
                 from_z(s, k)
         for s in order:
             for k in range(count):

time: 33.6 us -> 33.1 us (0.985)
  Pallas kernels: 33.4 us -> 33 us
    pallas_call x1, Pallas kernels: 19.5 us -> 19.1 us  [gather(): pl.pallas_call(gather_kernel, out_shape=jax.ShapeDtypeStruct((NEED, 16, 1...]
where the time goes in v5:
time: 33.1 us; the launch traced here: 33 us
  Pallas kernels  33 us (100%)
    pallas_call x1, Pallas kernels, gather(): pl.pallas_call(gather_kernel, out_shape=jax.ShapeDtypeStruct((NEED, 16, 1...  19.1 us
    pallas_call x1, Pallas kernels, cross(): pl.pallas_call(functools.partial(cross_kernel, 1.0 / windows), out_shape=...  13.9 us

profile of v5, /device:TPU:0, one launch (start us, length us, event | category | flops | bytes accessed | tf_op | source)
XLA Modules:
  0.0 33.0 jit_solution(5441740837331205762)
XLA Ops:
  0.0 19.1 %gather.1.h_ref = bf16[6,16,16,512]{3,2,1,0:T(8,128)(2,1)S(1)} custom-call(f32[2,2,2,8192]{3,2,1,0:T(2,128)} %x_hbm.1, s32[1,8192]{1,0:T(1,128)} %bitcast.2), custom_call_target="tpu_custom_call" | custom-call | tf_op jit(solution)/shard_map/gather/pallas_call | solution.py:236
  19.1 13.9 %cross.1 = f32[9,2,512,1024]{3,2,1,0:T(8,128)} custom-call(bf16[6,16,16,512]{3,2,1,0:T(8,128)(2,1)S(1)} %gather.1.h_ref), custom_call_target="tpu_custom_call" | custom-call | tf_op jit(solution)/shard_map/cross/pallas_call | solution.py:323
